TPU v7x, 32 devices: a whole 2x2x4 slice. The times are simulated.
32 devices in a mesh: frames: 2 (over core), phon: 4 (over y, x), chap: 4 (over z).
Axes of the slice: x: 2, y: 2, z: 4, core: 2. Of those that a mesh axis runs over, the one named last changes fastest.
Arguments:
- queries: bfloat16 [4096, 512], P(('chap', 'frames')), parts along dimension 0, may hold values from -80 to 80
- keys: bfloat16 [16384, 512], P(('chap', 'phon', 'frames')), parts along dimension 0, may hold values from -7 to 7
- values: bfloat16 [16384, 512], P(('chap', 'phon', 'frames')), parts along dimension 0, may hold values from -6 to 6
- band_first: int32 [8], P(('chap', 'frames')), parts along dimension 0, may hold values from 0 to 6, as said below
- cotangent: bfloat16 [4096, 512], P(('chap', 'frames')), parts along dimension 0, may hold values from -6 to 6
Outputs:
- aligned: bfloat16 [4096, 512], P(('chap', 'frames')), parts along dimension 0
- grad_query: bfloat16 [4096, 512], P(('chap', 'frames')), parts along dimension 0
- grad_key: float32 [16384, 512], P(('chap', 'phon', 'frames')), parts along dimension 0
- grad_value: float32 [16384, 512], P(('chap', 'phon', 'frames')), parts along dimension 0
There are 4 independent parts, one for each index of `chap`. A program takes and returns all parts, laid end to end along the dimension named above; each array names one. Nothing has to cross between parts.
Inputs may be any that keep to these rules, and one draw needn't show every extreme that they name: Query tile i attends the key tiles band_first[i] to band_first[i] + 1.
All inputs are finite; a program needn't handle non-finite values.
Results may differ from a plain program's by a relative error of at most 0.022.
Values may be sent and summed in bfloat16 or wider, within the bound.
A program may use at most 64 MiB of HBM per device.

v0:
```python
import jax
import jax.numpy as jnp
from jax import lax
from jax.sharding import PartitionSpec as P

TILE = 512
NBAND = 2


NEG_FILL = -1e30


def body(queries, keys, values, band_first, cotangent):
    width = queries.shape[1]
    scale = width ** (-0.5)
    block_keys, block_values = (
        lax.all_gather(keys, "frames", axis=0, tiled=True),
        lax.all_gather(values, "frames", axis=0, tiled=True),
    )
    block = block_keys.shape[0]
    first_tile = lax.axis_index("phon") * (block // TILE)
    key_tile = first_tile + jnp.arange(block, dtype=jnp.int32) // TILE
    row_first = jnp.repeat(band_first, TILE)
    allowed = (key_tile[None, :] >= row_first[:, None]) & (
        key_tile[None, :] < row_first[:, None] + NBAND
    )
    key_float = block_keys.astype(jnp.float32)
    key_sq = jnp.sum(key_float * key_float, axis=1)
    raw = (
        jnp.dot(queries, block_keys.T, preferred_element_type=jnp.float32) - 0.5 * key_sq[None, :]
    ) * scale
    scores = jnp.where(allowed, raw, NEG_FILL)
    local_max = jnp.max(scores, axis=1)
    row_max = lax.pmax(local_max, "phon")
    expd = jnp.where(allowed, jnp.exp(scores - row_max[:, None]), 0.0)
    part_total = jnp.sum(expd, axis=1)
    part_out = jnp.dot(expd.astype(jnp.bfloat16), block_values, preferred_element_type=jnp.float32)
    total, summed = lax.psum((part_total, part_out), "phon")
    aligned_f = summed / total[:, None]
    lse = row_max + jnp.log(total)
    back_keys, back_values = (block_keys, block_values)
    probs = jnp.where(allowed, jnp.exp(scores - lse[:, None]), 0.0)
    d_probs = jnp.dot(cotangent, back_values.T, preferred_element_type=jnp.float32)
    delta = jnp.sum(cotangent.astype(jnp.float32) * aligned_f, axis=1)
    d_scores = probs * (d_probs - delta[:, None])
    ds_low = d_scores.astype(jnp.bfloat16)
    part_query = jnp.dot(ds_low, back_keys, preferred_element_type=jnp.float32) * scale
    grad_query = lax.psum(part_query.astype(jnp.bfloat16), "phon")
    column_sum = jnp.sum(d_scores, axis=0)
    part_key = (
        jnp.einsum("qk,qd->kd", ds_low, queries, preferred_element_type=jnp.float32)
        - column_sum[:, None] * back_keys.astype(jnp.float32)
    ) * scale
    part_value = jnp.einsum(
        "qk,qd->kd", probs.astype(jnp.bfloat16), cotangent, preferred_element_type=jnp.float32
    )
    grad_key, grad_value = (
        lax.psum_scatter(
            part_key.astype(jnp.bfloat16), "frames", scatter_dimension=0, tiled=True
        ).astype(jnp.float32),
        lax.psum_scatter(
            part_value.astype(jnp.bfloat16), "frames", scatter_dimension=0, tiled=True
        ).astype(jnp.float32),
    )
    return (aligned_f.astype(jnp.bfloat16), grad_query, grad_key, grad_value)


def solution(mesh):
    in_specs = (
        P(("chap", "frames"), None),
        P(("chap", "phon", "frames"), None),
        P(("chap", "phon", "frames"), None),
        P(("chap", "frames")),
        P(("chap", "frames"), None),
    )
    out_specs = (
        P(("chap", "frames"), None),
        P(("chap", "frames"), None),
        P(("chap", "phon", "frames"), None),
        P(("chap", "phon", "frames"), None),
    )
    return jax.shard_map(body, mesh=mesh, in_specs=in_specs, out_specs=out_specs, check_vma=False)
```

profile of v0, /device:TPU:0, one launch (start us, length us, event | category | flops | bytes accessed | tf_op | source)
XLA Modules:
  0.0 172.3 jit_solution(3283855296457372618)
XLA Ops:
  7.2 0.7 all-gather.3.cloned.1.call-update
  8.0 0.7 all-gather.5.cloned.1.call-update
  9.4 12.0 %all-gather.3.cloned.1.call-done = bf16[1024,512]{1,0:T(8,128)(2,1)} async-done(((bf16[512,512]{1,0:T(8,128)(2,1)}), bf16[1024,512]{1,0:T(8,128)(2,1)}) %all-gather.3.cloned.1.call-update) | async-done | bytes 1048592 | tf_op jit(solution)/shard_map/all_gather | solution.py:17
  21.3 1.5 fusion
  22.9 2.1 %fusion.29 = (f32[512]{0:T(512)S(1)}, f32[512,1024]{1,0:T(8,128)S(1)}) fusion(f32[1024]{0:T(1024)S(1)} %broadcast_multiply_fusion, bf16[512,512]{1,0:T(8,128)(2,1)S(1)} %copy-done, bf16[1024,512]{1,0:T(8,128)(2,1)} %all-gather.3.cloned.1.call-done, pred[1024]{0:T(1024)(128)(4,1)S(1)} %fusion.25), kind=kOutput, calls=%fused_computation.43 | convolution fusion | flops 538967552 | bytes 3677184 | tf_op jit(solution)/shard_map/dot_general | solution.py:30
  24.9 10.1 %pmax.7 = f32[512]{0:T(512)S(1)} all-reduce(f32[512]{0:T(512)S(1)} %get-tuple-element.6), channel_id=1, replica_groups=mesh['frames'=2,'phon'=4,'chap'=4] {'phon'}, use_global_device_ids=true, to_apply=%region_2.3 | all-reduce | flops 512 | bytes 4096 | tf_op jit(solution)/shard_map/pmax | solution.py:34
  35.0 3.0 %fusion.9 = f32[512,512]{1,0:T(8,128)} fusion(bf16[1024,512]{1,0:T(8,128)(2,1)} %all-gather.5.cloned.1.call-done, f32[512,1024]{1,0:T(8,128)S(1)} %get-tuple-element.7, f32[512]{0:T(512)S(1)} %pmax.7, pred[1024]{0:T(1024)(128)(4,1)S(1)} %fusion.25), kind=kOutput, calls=%fused_computation.16 | convolution fusion | flops 538443776 | bytes 4197376 | tf_op jit(solution)/shard_map/dot_general | solution.py:37
  38.0 0.0 reduce-scatter.5.cloned.1.call-start
  38.1 0.5 fusion.4
  38.6 8.2 %psum.22 = f32[512]{0:T(512)S(1)} all-reduce(f32[512]{0:T(512)S(1)} %fusion.4), channel_id=1, replica_groups=mesh['frames'=2,'phon'=4,'chap'=4] {'phon'}, use_global_device_ids=true, to_apply=%region_5.6 | all-reduce | flops 512 | bytes 4096 | tf_op jit(solution)/shard_map/psum | solution.py:38
  46.9 1.9 %convolution_convert_fusion = bf16[1024,512]{1,0:T(8,128)(2,1)} fusion(bf16[512,512]{1,0:T(8,128)(2,1)S(1)} %copy-done.3, f32[512,1024]{1,0:T(8,128)S(1)} %get-tuple-element.7, f32[512]{0:T(512)S(1)} %log_add_fusion, pred[1024]{0:T(1024)(128)(4,1)S(1)} %fusion.25), kind=kOutput, calls=%fused_computation.13 | convolution fusion | flops 538968064 | bytes 3673088 | tf_op jit(solution)/shard_map/qk,qd->kd/dot_general | solution.py:54
  48.8 0.0 reduce-scatter.3.cloned.1.call-start
  48.8 41.7 %all-reduce.3.cloned.1.call-done = f32[512,512]{1,0:T(8,128)} async-done(((f32[512,512]{1,0:T(8,128)}), f32[512,512]{1,0:T(8,128)}) %all-reduce.3.cloned.1.call-update) | async-done | bytes 1048592 | tf_op jit(solution)/shard_map/psum | solution.py:38
  90.5 2.3 %multiply_reduce_fusion = (f32[512]{0:T(512)S(1)}, bf16[512,512]{1,0:T(8,128)(2,1)}) fusion(bf16[512,512]{1,0:T(8,128)(2,1)S(1)} %copy-done.3, f32[512,512]{1,0:T(8,128)} %all-reduce.3.cloned.1.call-done, f32[512]{0:T(512)S(1)} %psum.22), kind=kLoop, calls=%fused_computation.17 | loop fusion | flops 1310208 | bytes 2101248 | tf_op jit(solution)/shard_map/reduce_sum | solution.py:44
  92.8 0.8 fusion.30
  93.7 1.0 copy-done.5
  94.7 1.7 %fusion.3 = bf16[1024,512]{1,0:T(8,128)(2,1)} fusion(bf16[1024,512]{1,0:T(8,128)(2,1)S(1)} %copy-done.1, bf16[512,512]{1,0:T(8,128)(2,1)S(1)} %copy-done, f32[1024]{0:T(1024)S(1)} %get-tuple-element.8, bf16[512,1024]{1,0:T(8,128)(2,1)S(1)} %get-tuple-element.9), kind=kOutput, calls=%fused_computation.5 | convolution fusion | flops 539492352 | bytes 3674112 | tf_op jit(solution)/shard_map/qk,qd->kd/dot_general | solution.py:51
  96.5 2.7 %fusion.7 = bf16[512,512]{1,0:T(8,128)(2,1)} fusion(bf16[1024,512]{1,0:T(8,128)(2,1)S(1)} %copy-done.2, bf16[512,1024]{1,0:T(8,128)(2,1)} %copy-done.5), kind=kOutput, calls=%fused_computation.15 | convolution fusion | flops 537395200 | bytes 2621440 | tf_op jit(solution)/shard_map/dot_general | solution.py:47
  99.2 1.9 %reduce-scatter.5.cloned.1.call-done = bf16[512,512]{1,0:T(8,128)(2,1)} async-done(((bf16[1024,512]{1,0:T(8,128)(2,1)}), bf16[512,512]{1,0:T(8,128)(2,1)}) %reduce-scatter.5.cloned.1.call-update) | async-done | bytes 524304 | tf_op jit(solution)/shard_map/reduce_scatter | solution.py:61
  101.2 2.1 %convert_element_type.44 = f32[512,512]{1,0:T(8,128)} convert(bf16[512,512]{1,0:T(8,128)(2,1)} %reduce-scatter.5.cloned.1.call-done) | non-fusion elementwise | flops 262144 | bytes 1572864 | tf_op jit(solution)/shard_map/convert_element_type | solution.py:63
  103.3 10.3 %reduce-scatter.3.cloned.1.call-done = bf16[512,512]{1,0:T(8,128)(2,1)} async-done(((bf16[1024,512]{1,0:T(8,128)(2,1)}), bf16[512,512]{1,0:T(8,128)(2,1)}) %reduce-scatter.3.cloned.1.call-update) | async-done | bytes 524304 | tf_op jit(solution)/shard_map/reduce_scatter | solution.py:58
  113.7 2.1 %convert_element_type.41 = f32[512,512]{1,0:T(8,128)} convert(bf16[512,512]{1,0:T(8,128)(2,1)} %reduce-scatter.3.cloned.1.call-done) | non-fusion elementwise | flops 262144 | bytes 1572864 | tf_op jit(solution)/shard_map/convert_element_type | solution.py:60
  115.8 47.8 %all-reduce.5.cloned.1.call-done = bf16[512,512]{1,0:T(8,128)(2,1)} async-done(((bf16[512,512]{1,0:T(8,128)(2,1)}), bf16[512,512]{1,0:T(8,128)(2,1)}) %all-reduce.5.cloned.1.call-update) | async-done | bytes 524304 | tf_op jit(solution)/shard_map/psum | solution.py:48
  163.6 1.9 %copy.12 = bf16[512,512]{1,0:T(8,128)(2,1)} copy(bf16[512,512]{1,0:T(8,128)(2,1)} %all-reduce.5.cloned.1.call-done) | data formatting | bytes 1048576
  (23 shorter events, 0.3 us)
Async XLA Ops:
  7.2 15.7 %copy-start = (bf16[512,512]{1,0:T(8,128)(2,1)S(1)}, bf16[512,512]{1,0:T(8,128)(2,1)}, u32[]{:S(2)}) copy-start(bf16[512,512]{1,0:T(8,128)(2,1)} %param.5) | copy-start | bytes 1572868
  7.2 14.1 %all-gather.3.cloned.1.call-start = ((), (), s32[]{:S(2)}) async-start(), calls=%async_computation.2 | async-start | bytes 1572864 | tf_op jit(solution)/shard_map/all_gather | solution.py:17
  7.9 27.1 %all-gather.5.cloned.1.call-start = ((), (), s32[]{:S(2)}) async-start(), calls=%async_computation.3 | async-start | bytes 1572864 | tf_op jit(solution)/shard_map/all_gather | solution.py:18
  8.7 81.8 %all-reduce.3.cloned.1.call-start = ((), (), s32[]{:S(2)}) async-start(), calls=%async_computation.4 | async-start | bytes 2097152 | tf_op jit(solution)/shard_map/psum | solution.py:38
  38.0 8.9 %copy-start.3 = (bf16[512,512]{1,0:T(8,128)(2,1)S(1)}, bf16[512,512]{1,0:T(8,128)(2,1)}, u32[]{:S(2)}) copy-start(bf16[512,512]{1,0:T(8,128)(2,1)} %param.9) | copy-start | bytes 1572868
  38.0 63.1 %reduce-scatter.5.cloned.1.call-start = ((), (), s32[]{:S(2)}) async-start(), calls=%async_computation.7 | async-start | bytes 1572864 | tf_op jit(solution)/shard_map/reduce_scatter | solution.py:61
  48.8 64.9 %reduce-scatter.3.cloned.1.call-start = ((), (), s32[]{:S(2)}) async-start(), calls=%async_computation.6 | async-start | bytes 1572864 | tf_op jit(solution)/shard_map/reduce_scatter | solution.py:58
  90.5 2.3 %copy-start.4 = (bf16[1024,512]{1,0:T(8,128)(2,1)S(1)}, bf16[1024,512]{1,0:T(8,128)(2,1)}, u32[]{:S(2)}) copy-start(bf16[1024,512]{1,0:T(8,128)(2,1)} %all-gather.5.cloned.1.call-done) | copy-start | bytes 3145732
  92.8 1.8 %copy-start.1 = (bf16[1024,512]{1,0:T(8,128)(2,1)S(1)}, bf16[1024,512]{1,0:T(8,128)(2,1)}, u32[]{:S(2)}) copy-start(bf16[1024,512]{1,0:T(8,128)(2,1)} %all-gather.3.cloned.1.call-done) | copy-start | bytes 3145732
  93.7 1.0 copy-start.5
  94.7 1.8 %copy-start.2 = (bf16[1024,512]{1,0:T(8,128)(2,1)S(1)}, bf16[1024,512]{1,0:T(8,128)(2,1)}, u32[]{:S(2)}) copy-start(bf16[1024,512]{1,0:T(8,128)(2,1)} %all-gather.3.cloned.1.call-done) | copy-start | bytes 3145732
  96.4 67.2 %all-reduce.5.cloned.1.call-start = ((), (), s32[]{:S(2)}) async-start(), calls=%async_computation.5 | async-start | bytes 1048576 | tf_op jit(solution)/shard_map/psum | solution.py:48
Sparse Core Ops, SparseCore 0:
  9.6 11.7 all-gather.2
  22.9 10.1 all-gather.4
  38.2 52.2 all-reduce.2
  92.6 8.5 reduce-scatter.4
  103.9 9.6 reduce-scatter.2
  117.1 46.5 all-reduce.4
where the time goes:
time: 173 us; the launch traced here: 172 us
  waiting for transfers between devices  115 us (66%)
  blocking collectives  18.3 us (11%)
  between operations  14.8 us (9%)
  matrix products  12.2 us (7%)
  other arithmetic  8.65 us (5%)
  local copies, waits for them, and re-layouts  2.86 us (2%)
    psum x1, waiting for transfers between devices, body(): grad_query = lax.psum(part_query.astype(jnp.bfloat16), 'phon')  47.8 us
    psum x1, waiting for transfers between devices, body(): total, summed = lax.psum((part_total, part_out), 'phon')  41.7 us
    all_gather x1, waiting for transfers between devices, body(): lax.all_gather(keys, 'frames', axis=0, tiled=True)  12 us
    reduce_scatter x1, waiting for transfers between devices, body(): lax.psum_scatter(part_key.astype(jnp.bfloat16), 'frames', scatter_dimensi...  10.3 us
    pmax x1, blocking collectives, body(): row_max = lax.pmax(local_max, 'phon')  10.1 us
    psum x1, blocking collectives, body(): total, summed = lax.psum((part_total, part_out), 'phon')  8.25 us
    convert_element_type x2, other arithmetic, body(): grad_key, grad_value = (lax.psum_scatter(part_key.astype(jnp.bfloat16), '...  4.29 us
  transfers between devices with their start and end apart: 6, of which 5 were waited for; matrix products, arithmetic and copies ran while one was open for 10% of the time, Pallas kernels for 0%

commit v1 on v0

v1 whole, which is shorter than its diff:
```python
import functools

import jax
import jax.numpy as jnp
from jax import lax
from jax.experimental import pallas as pl
from jax.experimental.pallas import tpu as pltpu
from jax.sharding import PartitionSpec as P

TILE = 512
NBAND = 2
NEG_FILL = -1e30
STEP = 256

F32 = jnp.float32
BF16 = jnp.bfloat16


def dot(a, b, ca, cb):
    return lax.dot_general(a, b, (((ca,), (cb,)), ((), ())), preferred_element_type=F32)


def kernel(
    nf, nphon,
    band, q_hbm, k_hbm, v_hbm, g_hbm,
    al_out, gq_out, gk_out, gv_out,
    q, g, k, v, s, dp, prob, ds, o_part, gq_part, gk_part, gv_part,
    stat, stat_in, o_in, gq_in, gk_in, gv_in,
    local_sem, k_send, k_recv, v_send, v_recv, st_send, st_recv,
    o_send, o_recv, oa_send, oa_recv, q_send, q_recv, qa_send, qa_recv,
    gk_send, gk_recv, gv_send, gv_recv,
):
    f = lax.axis_index("frames")
    p = lax.axis_index("phon")
    nq, width = q.shape
    rows = k_hbm.shape[0]
    block = nf * rows
    part = nq // nphon
    scale = width ** (-0.5)

    def fdev(d):
        return {"frames": lax.rem(f + d + nf, nf)}

    def pdev(d):
        return {"phon": lax.rem(p + d, nphon)}

    def remote(src, dst, send, recv, dev):
        return pltpu.make_async_remote_copy(
            src_ref=src, dst_ref=dst, send_sem=send, recv_sem=recv,
            device_id=dev, device_id_type=pl.DeviceIdType.MESH,
        )

    loads = [
        pltpu.make_async_copy(k_hbm, k.at[pl.ds(0, rows)], local_sem.at[0]),
        pltpu.make_async_copy(q_hbm, q, local_sem.at[1]),
        pltpu.make_async_copy(v_hbm, v.at[pl.ds(0, rows)], local_sem.at[2]),
        pltpu.make_async_copy(g_hbm, g, local_sem.at[3]),
    ]
    for c in loads:
        c.start()

    barrier = pltpu.get_barrier_semaphore()
    for d in range(1, nf):
        pl.semaphore_signal(barrier, inc=1, device_id=fdev(d), device_id_type=pl.DeviceIdType.MESH)
    for d in range(1, nphon):
        pl.semaphore_signal(barrier, inc=1, device_id=pdev(d), device_id_type=pl.DeviceIdType.MESH)
    pl.semaphore_wait(barrier, nf - 1 + nphon - 1)

    pulls = []
    for d in range(1, nf):
        slot = pl.ds(d * rows, rows)
        pulls.append(remote(k_hbm, k.at[slot], k_send.at[d - 1], k_recv.at[d - 1], fdev(d)))
        pulls.append(remote(v_hbm, v.at[slot], v_send.at[d - 1], v_recv.at[d - 1], fdev(d)))
    for c in pulls:
        c.start()

    lane_tile = lax.broadcasted_iota(jnp.int32, (1, nq), 1) // TILE
    first = jnp.zeros((1, nq), jnp.int32)
    for i in range(band.shape[0]):
        first = jnp.where(lane_tile == i, band[i], first)
    ones = jnp.ones((8, width), BF16)

    def scores(t, top):
        r = pl.ds(pl.multiple_of(t * STEP, STEP), STEP)
        kt = k[r, :]
        row = t * STEP + lax.broadcasted_iota(jnp.int32, (STEP, 1), 0)
        src = lax.rem(f - row // rows + nf, nf)
        tile = (p * block + src * rows + lax.rem(row, rows)) // TILE
        kf = kt.astype(F32)
        sq = jnp.sum(kf * kf, axis=1, keepdims=True)
        raw = (dot(kt, q[...], 1, 1) - 0.5 * sq) * scale
        st = jnp.where((tile >= first) & (tile < first + NBAND), raw, NEG_FILL)
        s[r, :] = st
        dp[r, :] = dot(v[r, :], g[...], 1, 1)
        return jnp.maximum(top, jnp.max(st.reshape(STEP // 8, 8, nq), axis=0))

    top = jnp.full((8, nq), NEG_FILL, F32)
    near = rows // STEP if rows % STEP == 0 else 0
    for c in loads:
        c.wait()
    top = lax.fori_loop(0, near, scores, top)
    for c in pulls:
        c.wait_recv()
    top = lax.fori_loop(near, block // STEP, scores, top)
    top = jnp.max(top, axis=0, keepdims=True)

    def expand(t, carry):
        tot, mix = carry
        r = pl.ds(pl.multiple_of(t * STEP, STEP), STEP)
        e = jnp.exp(s[r, :] - top)
        s[r, :] = e
        tot = tot + jnp.sum(e.reshape(STEP // 8, 8, nq), axis=0)
        mix = mix + jnp.sum((e * dp[r, :]).reshape(STEP // 8, 8, nq), axis=0)
        return tot, mix

    zero = jnp.zeros((8, nq), F32)
    tot, mix = lax.fori_loop(0, block // STEP, expand, (zero, zero))
    tot = jnp.sum(tot, axis=0, keepdims=True)
    mix = jnp.sum(mix, axis=0, keepdims=True)
    stat[0:1, :] = top
    stat[1:2, :] = tot
    stat[2:3, :] = mix
    stat[3:8, :] = jnp.zeros((5, nq), F32)
    stats = [
        remote(stat, stat_in.at[d - 1], st_send.at[d - 1], st_recv.at[d - 1], pdev(d))
        for d in range(1, nphon)
    ]
    for c in stats:
        c.start()
    for c in stats:
        c.wait_recv()
    all_top = top
    for d in range(1, nphon):
        all_top = jnp.maximum(all_top, stat_in[d - 1, 0:1, :])
    mine = jnp.exp(top - all_top)
    total = tot * mine
    delta = mix * mine
    for d in range(1, nphon):
        w = jnp.exp(stat_in[d - 1, 0:1, :] - all_top)
        total = total + stat_in[d - 1, 1:2, :] * w
        delta = delta + stat_in[d - 1, 2:3, :] * w
    delta = delta / total
    mine = mine / total

    def soften(t, carry):
        r = pl.ds(pl.multiple_of(t * STEP, STEP), STEP)
        pt = s[r, :] * mine
        prob[r, :] = pt.astype(BF16)
        d_s = pt * (dp[r, :] - delta)
        dp[r, :] = d_s
        ds[r, :] = d_s.astype(BF16)
        return carry

    lax.fori_loop(0, block // STEP, soften, 0)

    def sends(part_ref, in_ref, send, recv):
        out = []
        for d in range(1, nphon):
            j = lax.rem(p + d, nphon)
            r = pl.ds(pl.multiple_of(j * part, part), part)
            out.append(remote(part_ref.at[r], in_ref.at[d - 1], send.at[d - 1], recv.at[d - 1], pdev(d)))
        return out

    o_part[...] = dot(prob[...], v[...], 0, 0).astype(BF16)
    o_rs = sends(o_part, o_in, o_send, o_recv)
    for c in o_rs:
        c.start()
    gq_part[...] = (dot(ds[...], k[...], 0, 0) * scale).astype(BF16)
    q_rs = sends(gq_part, gq_in, q_send, q_recv)
    for c in q_rs:
        c.start()

    def key_grads(t, carry):
        t = lax.rem(t + near, block // STEP)
        r = pl.ds(pl.multiple_of(t * STEP, STEP), STEP)
        col = jnp.sum(dp[r, :], axis=1, keepdims=True)
        gk = (dot(ds[r, :], q[...], 1, 0) - col * k[r, :].astype(F32)) * scale
        gk_part[r, :] = gk.astype(BF16)
        gv_part[r, :] = dot(prob[r, :], g[...], 1, 0).astype(BF16)
        return carry

    far = block // STEP - near
    lax.fori_loop(0, far, key_grads, 0)
    back = []
    for d in range(1, nf):
        slot = pl.ds(d * rows, rows)
        back.append(remote(gk_part.at[slot], gk_in.at[d - 1], gk_send.at[d - 1], gk_recv.at[d - 1], fdev(-d)))
        back.append(remote(gv_part.at[slot], gv_in.at[d - 1], gv_send.at[d - 1], gv_recv.at[d - 1], fdev(-d)))
    for c in back:
        c.start()
    lax.fori_loop(far, block // STEP, key_grads, 0)

    own = pl.ds(pl.multiple_of(p * part, part), part)

    def spread(rs, part_ref, in_ref, out_ref, send, recv):
        for c in rs:
            c.wait_recv()
        acc = part_ref[own, :].astype(F32)
        for d in range(1, nphon):
            acc = acc + in_ref[d - 1].astype(F32)
        out_ref[own, :] = acc.astype(BF16)
        ag = [
            remote(out_ref.at[own], out_ref.at[own], send.at[d - 1], recv.at[d - 1], pdev(d))
            for d in range(1, nphon)
        ]
        for c in ag:
            c.start()
        return ag

    o_ag = spread(o_rs, o_part, o_in, al_out, oa_send, oa_recv)
    q_ag = spread(q_rs, gq_part, gq_in, gq_out, qa_send, qa_recv)

    for c in back:
        c.wait_recv()
    gk = gk_part[pl.ds(0, rows), :].astype(F32)
    gv = gv_part[pl.ds(0, rows), :].astype(F32)
    for d in range(1, nf):
        gk = gk + gk_in[d - 1].astype(F32)
        gv = gv + gv_in[d - 1].astype(F32)
    gk_out[...] = gk
    gv_out[...] = gv

    for c in o_ag + q_ag:
        c.wait_recv()
    for c in pulls + stats + o_rs + q_rs + back + o_ag + q_ag:
        c.wait_send()


def body(nf, nphon, queries, keys, values, band_first, cotangent):
    nq, width = queries.shape
    rows = keys.shape[0]
    block = rows * nf
    part = nq // nphon
    hbm = pl.BlockSpec(memory_space=pl.ANY)
    vmem = pl.BlockSpec(memory_space=pltpu.VMEM)
    dma = pltpu.SemaphoreType.DMA
    return pl.pallas_call(
        functools.partial(kernel, nf, nphon),
        out_shape=(
            jax.ShapeDtypeStruct((nq, width), BF16),
            jax.ShapeDtypeStruct((nq, width), BF16),
            jax.ShapeDtypeStruct((rows, width), F32),
            jax.ShapeDtypeStruct((rows, width), F32),
        ),
        in_specs=[pl.BlockSpec(memory_space=pltpu.SMEM), hbm, hbm, hbm, hbm],
        out_specs=(vmem,) * 4,
        scratch_shapes=[
            pltpu.VMEM((nq, width), BF16),
            pltpu.VMEM((nq, width), BF16),
            pltpu.VMEM((block, width), BF16),
            pltpu.VMEM((block, width), BF16),
            pltpu.VMEM((block, nq), F32),
            pltpu.VMEM((block, nq), F32),
            pltpu.VMEM((block, nq), BF16),
            pltpu.VMEM((block, nq), BF16),
            pltpu.VMEM((nq, width), BF16),
            pltpu.VMEM((nq, width), BF16),
            pltpu.VMEM((block, width), BF16),
            pltpu.VMEM((block, width), BF16),
            pltpu.VMEM((8, nq), F32),
            pltpu.VMEM((nphon - 1, 8, nq), F32),
            pltpu.VMEM((nphon - 1, part, width), BF16),
            pltpu.VMEM((nphon - 1, part, width), BF16),
            pltpu.VMEM((nf - 1, rows, width), BF16),
            pltpu.VMEM((nf - 1, rows, width), BF16),
            dma((4,)),
        ]
        + [dma((nf - 1,))] * 4
        + [dma((nphon - 1,))] * 10
        + [dma((nf - 1,))] * 4,
        compiler_params=pltpu.CompilerParams(
            collective_id=0, has_side_effects=True, vmem_limit_bytes=48 * 2**20
        ),
    )(band_first, queries, keys, values, cotangent)


def solution(mesh):
    tile = P(("chap", "frames"), None)
    key = P(("chap", "phon", "frames"), None)
    return jax.shard_map(
        functools.partial(body, mesh.shape["frames"], mesh.shape["phon"]),
        mesh=mesh,
        in_specs=(tile, key, key, P(("chap", "frames")), tile),
        out_specs=(tile, tile, key, key),
        check_vma=False,
    )
```

time: 173 us -> 46 us (0.27)
  waiting for transfers between devices: 115 us -> 0 us
  Pallas kernels: 0 us -> 36.7 us
  blocking collectives: 18.3 us -> 0 us
  between operations: 14.8 us -> 1.3 us
  matrix products: 12.2 us -> 0 us
  other arithmetic: 8.65 us -> 0 us
  local copies, waits for them, and re-layouts: 2.86 us -> 7.69 us
    psum x2 -> x0, waiting for transfers between devices: 89.5 us -> none  [the longest x1 47.8 us: body(): grad_query = lax.psum(part_query.astype(jnp.bfloat16), 'phon')]
    pallas_call x0 -> x1, Pallas kernels: none -> 36.7 us  [body(): pl.pallas_call(functools.partial(kernel, nf, nphon), out_shape=(jax.Shape...]
    reduce_scatter x2 -> x0, waiting for transfers between devices: 12.3 us -> none  [the longest x1 10.3 us: body(): lax.psum_scatter(part_key.astype(jnp.bfloat16), 'frames', scatter_dimensi...]
    dot_general x6 -> x0, matrix products: 12.2 us -> none  [the longest x1 2.97 us: body(): jnp.dot(expd.astype(jnp.bfloat16), block_values, preferred_element_type=j...]
    all_gather x2 -> x0, waiting for transfers between devices: 12 us -> none  [the longest x1 12 us: body(): lax.all_gather(keys, 'frames', axis=0, tiled=True)]
    pmax x1 -> x0, blocking collectives: 10.1 us -> none  [body(): row_max = lax.pmax(local_max, 'phon')]
    psum x1 -> x0, blocking collectives: 8.25 us -> none  [body(): total, summed = lax.psum((part_total, part_out), 'phon')]
    unnamed x13 -> x12, local copies, waits for them, and re-layouts: 2.86 us -> 7.69 us
  transfers between devices with their start and end apart: 6 -> 0, of which waited for: 5 -> 0; matrix products, arithmetic and copies ran while one was open for 10% -> 0% of each run, Pallas kernels for 0% -> 0%
where the time goes in v1:
time: 46 us; the launch traced here: 45.7 us
  Pallas kernels  36.7 us (80%)
  local copies, waits for them, and re-layouts  7.69 us (17%)
  between operations  1.3 us (3%)
    pallas_call x1, Pallas kernels, body(): pl.pallas_call(functools.partial(kernel, nf, nphon), out_shape=(jax.Shape...  36.7 us
    unnamed x12, local copies, waits for them, and re-layouts  7.69 us

profile of v1, /device:TPU:0, one launch (start us, length us, event | category | flops | bytes accessed | tf_op | source)
XLA Modules:
  0.0 45.7 jit_solution(8461523165751328027)
XLA Ops:
  1.3 0.0 copy-start
  1.3 1.0 %copy-done = bf16[512,512]{1,0:T(8,128)(2,1)S(1)} copy-done((bf16[512,512]{1,0:T(8,128)(2,1)S(1)}, bf16[512,512]{1,0:T(8,128)(2,1)}, u32[]{:S(2)}) %copy-start) | copy-done | bytes 524312
  2.3 0.0 copy-start.1
  2.3 1.0 %copy-done.1 = bf16[512,512]{1,0:T(8,128)(2,1)S(1)} copy-done((bf16[512,512]{1,0:T(8,128)(2,1)S(1)}, bf16[512,512]{1,0:T(8,128)(2,1)}, u32[]{:S(2)}) %copy-start.1) | copy-done | bytes 524312
  3.4 0.0 copy-start.2
  3.4 1.0 %copy-done.2 = bf16[512,512]{1,0:T(8,128)(2,1)S(1)} copy-done((bf16[512,512]{1,0:T(8,128)(2,1)S(1)}, bf16[512,512]{1,0:T(8,128)(2,1)}, u32[]{:S(2)}) %copy-start.2) | copy-done | bytes 524312
  4.4 0.0 copy-start.3
  4.4 1.0 %copy-done.3 = bf16[512,512]{1,0:T(8,128)(2,1)S(1)} copy-done((bf16[512,512]{1,0:T(8,128)(2,1)S(1)}, bf16[512,512]{1,0:T(8,128)(2,1)}, u32[]{:S(2)}) %copy-start.3) | copy-done | bytes 524312
  5.4 36.7 %shard_map.84 = (bf16[512,512]{1,0:T(8,128)(2,1)S(1)}, bf16[512,512]{1,0:T(8,128)(2,1)S(1)}, f32[512,512]{1,0:T(8,128)S(1)}, f32[512,512]{1,0:T(8,128)S(1)}) custom-call(s32[1]{0:T(128)S(6)} %copy.13.band, bf16[512,512]{1,0:T(8,128)(2,1)S(1)} %copy-done, bf16[512,512]{1,0:T(8,128)(2,1)S(1)} %copy-done.1, bf16[512,512]{1,0:T(8,128)(2,1)S(1)} %copy-done.2, ...), custom_call_target="tpu_custom_call" | custom-call | tf_op jit(solution)/shard_map/pallas_call | solution.py:237
  42.2 0.8 %copy.14 = bf16[512,512]{1,0:T(8,128)(2,1)} copy(bf16[512,512]{1,0:T(8,128)(2,1)S(1)} %get-tuple-element.8) | data formatting | bytes 1048576
  43.0 0.8 %copy.15 = bf16[512,512]{1,0:T(8,128)(2,1)} copy(bf16[512,512]{1,0:T(8,128)(2,1)S(1)} %get-tuple-element.9) | data formatting | bytes 1048576
  43.8 1.0 %copy.16 = f32[512,512]{1,0:T(8,128)} copy(f32[512,512]{1,0:T(8,128)S(1)} %get-tuple-element.10) | data formatting | bytes 2097152
  44.7 1.0 %copy.17 = f32[512,512]{1,0:T(8,128)} copy(f32[512,512]{1,0:T(8,128)S(1)} %get-tuple-element.11) | data formatting | bytes 2097152
Async XLA Ops:
  1.3 1.0 %copy-start = (bf16[512,512]{1,0:T(8,128)(2,1)S(1)}, bf16[512,512]{1,0:T(8,128)(2,1)}, u32[]{:S(2)}) copy-start(bf16[512,512]{1,0:T(8,128)(2,1)} %q_hbm.1) | copy-start | bytes 1572868
  2.3 1.0 %copy-start.1 = (bf16[512,512]{1,0:T(8,128)(2,1)S(1)}, bf16[512,512]{1,0:T(8,128)(2,1)}, u32[]{:S(2)}) copy-start(bf16[512,512]{1,0:T(8,128)(2,1)} %k_hbm.1) | copy-start | bytes 1572868
  3.4 1.0 %copy-start.2 = (bf16[512,512]{1,0:T(8,128)(2,1)S(1)}, bf16[512,512]{1,0:T(8,128)(2,1)}, u32[]{:S(2)}) copy-start(bf16[512,512]{1,0:T(8,128)(2,1)} %v_hbm.1) | copy-start | bytes 1572868
  4.4 1.0 %copy-start.3 = (bf16[512,512]{1,0:T(8,128)(2,1)S(1)}, bf16[512,512]{1,0:T(8,128)(2,1)}, u32[]{:S(2)}) copy-start(bf16[512,512]{1,0:T(8,128)(2,1)} %g_hbm.1) | copy-start | bytes 1572868

commit v2 on v1

--- a/solution.py
+++ b/solution.py
@@ -23,11 +23,12 @@
 def kernel(
     nf, nphon,
     band, q_hbm, k_hbm, v_hbm, g_hbm,
+    al_hbm, gq_hbm, gk_hbm, gv_hbm,
     al_out, gq_out, gk_out, gv_out,
     q, g, k, v, s, dp, prob, ds, o_part, gq_part, gk_part, gv_part,
-    stat, stat_in, o_in, gq_in, gk_in, gv_in,
-    local_sem, k_send, k_recv, v_send, v_recv, st_send, st_recv,
-    o_send, o_recv, oa_send, oa_recv, q_send, q_recv, qa_send, qa_recv,
+    stat, stat_in, o_in1, o_sum, o_in2, q_in1, q_sum, q_in2, gk_in, gv_in,
+    local_sem, store_sem, k_send, k_recv, v_send, v_recv, st_send, st_recv,
+    o_send, o_recv, q_send, q_recv,
     gk_send, gk_recv, gv_send, gv_recv,
 ):
     f = lax.axis_index("frames")
@@ -35,7 +36,6 @@
     nq, width = q.shape
     rows = k_hbm.shape[0]
     block = nf * rows
-    part = nq // nphon
     scale = width ** (-0.5)
 
     def fdev(d):
@@ -153,22 +153,75 @@
 
     lax.fori_loop(0, block // STEP, soften, 0)
 
-    def sends(part_ref, in_ref, send, recv):
+    x, y = lax.rem(p, 2), p // 2
+    xdev = {"phon": y * 2 + 1 - x}
+    ydev = {"phon": (1 - y) * 2 + x}
+    half, quarter, eighth = nq // 2, nq // 4, nq // 8
+
+    def at(offset, size, unit):
+        return pl.ds(pl.multiple_of(offset, unit), size)
+
+    def first_step(part_ref, in1, send, recv):
+        copies = [
+            remote(part_ref.at[at((1 - x) * quarter, quarter, quarter)], in1.at[0], send.at[0], recv.at[0], xdev),
+            remote(part_ref.at[at(half + (1 - y) * quarter, quarter, quarter)], in1.at[1], send.at[1], recv.at[1], ydev),
+        ]
+        for c in copies:
+            c.start()
+        return copies
+
+    def second_step(copies, part_ref, in1, sum1, in2, send, recv):
         out = []
-        for d in range(1, nphon):
-            j = lax.rem(p + d, nphon)
-            r = pl.ds(pl.multiple_of(j * part, part), part)
-            out.append(remote(part_ref.at[r], in_ref.at[d - 1], send.at[d - 1], recv.at[d - 1], pdev(d)))
+        for i, (base, near_bit, far_dev) in enumerate(((x * quarter, y, ydev), (half + y * quarter, x, xdev))):
+            copies[i].wait_recv()
+            both = part_ref[at(base, quarter, quarter), :].astype(F32) + in1[i].astype(F32)
+            sum1[i] = both.astype(BF16)
+            c = remote(
+                sum1.at[i, at((1 - near_bit) * eighth, eighth, eighth)], in2.at[i],
+                send.at[2 + i], recv.at[2 + i], far_dev,
+            )
+            c.start()
+            out.append(c)
         return out
 
+    def rows_of(px, py):
+        return (
+            at(px * quarter + py * eighth, eighth, eighth),
+            at(half + py * quarter + px * eighth, eighth, eighth),
+        )
+
+    def third_step(copies, sum1, in2, out_ref, send, recv):
+        mine_rows = rows_of(x, y)
+        out = []
+        for i, near_bit in enumerate((y, x)):
+            copies[i].wait_recv()
+            total_rows = sum1[i, at(near_bit * eighth, eighth, eighth), :].astype(F32) + in2[i].astype(F32)
+            out_ref[mine_rows[i], :] = total_rows.astype(BF16)
+            view = out_ref.at[mine_rows[i]]
+            for j, dev in enumerate((xdev, ydev)):
+                n = 4 + 2 * i + j
+                c = remote(view, view, send.at[n], recv.at[n], dev)
+                c.start()
+                out.append(c)
+        return out
+
+    def fourth_step(copies, out_ref, send, recv):
+        out = []
+        copies[1].wait_recv()
+        view = out_ref.at[rows_of(x, 1 - y)[0]]
+        out.append(remote(view, view, send.at[8], recv.at[8], xdev))
+        out[0].start()
+        copies[2].wait_recv()
+        view = out_ref.at[rows_of(1 - x, y)[1]]
+        out.append(remote(view, view, send.at[9], recv.at[9], ydev))
+        out[1].start()
+        return out
+
     o_part[...] = dot(prob[...], v[...], 0, 0).astype(BF16)
-    o_rs = sends(o_part, o_in, o_send, o_recv)
-    for c in o_rs:
-        c.start()
+    o_1 = first_step(o_part, o_in1, o_send, o_recv)
     gq_part[...] = (dot(ds[...], k[...], 0, 0) * scale).astype(BF16)
-    q_rs = sends(gq_part, gq_in, q_send, q_recv)
-    for c in q_rs:
-        c.start()
+    q_1 = first_step(gq_part, q_in1, q_send, q_recv)
+    o_2 = second_step(o_1, o_part, o_in1, o_sum, o_in2, o_send, o_recv)
 
     def key_grads(t, carry):
         t = lax.rem(t + near, block // STEP)
@@ -190,25 +243,10 @@
         c.start()
     lax.fori_loop(far, block // STEP, key_grads, 0)
 
-    own = pl.ds(pl.multiple_of(p * part, part), part)
-
-    def spread(rs, part_ref, in_ref, out_ref, send, recv):
-        for c in rs:
-            c.wait_recv()
-        acc = part_ref[own, :].astype(F32)
-        for d in range(1, nphon):
-            acc = acc + in_ref[d - 1].astype(F32)
-        out_ref[own, :] = acc.astype(BF16)
-        ag = [
-            remote(out_ref.at[own], out_ref.at[own], send.at[d - 1], recv.at[d - 1], pdev(d))
-            for d in range(1, nphon)
-        ]
-        for c in ag:
-            c.start()
-        return ag
-
-    o_ag = spread(o_rs, o_part, o_in, al_out, oa_send, oa_recv)
-    q_ag = spread(q_rs, gq_part, gq_in, gq_out, qa_send, qa_recv)
+    q_2 = second_step(q_1, gq_part, q_in1, q_sum, q_in2, q_send, q_recv)
+    o_3 = third_step(o_2, o_sum, o_in2, al_out, o_send, o_recv)
+    q_3 = third_step(q_2, q_sum, q_in2, gq_out, q_send, q_recv)
+    o_4 = fourth_step(o_3, al_out, o_send, o_recv)
 
     for c in back:
         c.wait_recv()
@@ -219,22 +257,44 @@
         gv = gv + gv_in[d - 1].astype(F32)
     gk_out[...] = gk
     gv_out[...] = gv
-
-    for c in o_ag + q_ag:
-        c.wait_recv()
-    for c in pulls + stats + o_rs + q_rs + back + o_ag + q_ag:
+    stores = [
+        pltpu.make_async_copy(gk_out, gk_hbm, store_sem.at[0]),
+        pltpu.make_async_copy(gv_out, gv_hbm, store_sem.at[1]),
+        pltpu.make_async_copy(al_out, al_hbm, store_sem.at[2]),
+        pltpu.make_async_copy(gq_out, gq_hbm, store_sem.at[3]),
+    ]
+    stores[0].start()
+    stores[1].start()
+
+    q_4 = fourth_step(q_3, gq_out, q_send, q_recv)
+    for copies, last, out in ((o_3, o_4, stores[2]), (q_3, q_4, stores[3])):
+        copies[0].wait_recv()
+        copies[3].wait_recv()
+        for c in last:
+            c.wait_recv()
+        out.start()
+    for c in pulls + stats + back + o_1 + o_2 + o_3 + o_4 + q_1 + q_2 + q_3 + q_4:
         c.wait_send()
+    for c in stores:
+        c.wait()
+
+
+def store(*refs):
+    n = len(refs) // 2
+    copies = [pltpu.make_async_copy(refs[i], refs[n + i], refs[-1].at[i]) for i in range(n)]
+    for c in copies:
+        c.start()
+    for c in copies:
+        c.wait()
 
 
 def body(nf, nphon, queries, keys, values, band_first, cotangent):
     nq, width = queries.shape
     rows = keys.shape[0]
     block = rows * nf
-    part = nq // nphon
     hbm = pl.BlockSpec(memory_space=pl.ANY)
-    vmem = pl.BlockSpec(memory_space=pltpu.VMEM)
     dma = pltpu.SemaphoreType.DMA
-    return pl.pallas_call(
+    results = pl.pallas_call(
         functools.partial(kernel, nf, nphon),
         out_shape=(
             jax.ShapeDtypeStruct((nq, width), BF16),
@@ -243,8 +303,12 @@
             jax.ShapeDtypeStruct((rows, width), F32),
         ),
         in_specs=[pl.BlockSpec(memory_space=pltpu.SMEM), hbm, hbm, hbm, hbm],
-        out_specs=(vmem,) * 4,
+        out_specs=(hbm,) * 4,
         scratch_shapes=[
+            pltpu.VMEM((nq, width), BF16),
+            pltpu.VMEM((nq, width), BF16),
+            pltpu.VMEM((rows, width), F32),
+            pltpu.VMEM((rows, width), F32),
             pltpu.VMEM((nq, width), BF16),
             pltpu.VMEM((nq, width), BF16),
             pltpu.VMEM((block, width), BF16),
@@ -259,19 +323,33 @@
             pltpu.VMEM((block, width), BF16),
             pltpu.VMEM((8, nq), F32),
             pltpu.VMEM((nphon - 1, 8, nq), F32),
-            pltpu.VMEM((nphon - 1, part, width), BF16),
-            pltpu.VMEM((nphon - 1, part, width), BF16),
+        ]
+        + [
+            pltpu.VMEM((2, nq // 4, width), BF16),
+            pltpu.VMEM((2, nq // 4, width), BF16),
+            pltpu.VMEM((2, nq // 8, width), BF16),
+        ] * 2
+        + [
             pltpu.VMEM((nf - 1, rows, width), BF16),
             pltpu.VMEM((nf - 1, rows, width), BF16),
             dma((4,)),
+            dma((4,)),
         ]
         + [dma((nf - 1,))] * 4
-        + [dma((nphon - 1,))] * 10
+        + [dma((nphon - 1,))] * 2
+        + [dma((10,))] * 4
         + [dma((nf - 1,))] * 4,
         compiler_params=pltpu.CompilerParams(
-            collective_id=0, has_side_effects=True, vmem_limit_bytes=48 * 2**20
+            collective_id=0, has_side_effects=True, vmem_limit_bytes=60 * 2**20
         ),
     )(band_first, queries, keys, values, cotangent)
+    return pl.pallas_call(
+        store,
+        out_shape=tuple(jax.ShapeDtypeStruct(r.shape, r.dtype) for r in results),
+        in_specs=[hbm] * 4,
+        out_specs=(hbm,) * 4,
+        scratch_shapes=[dma((4,))],
+    )(*results)
 
 
 def solution(mesh):

time: 46 us -> 132 us (2.87)
  Pallas kernels: 36.7 us -> 131 us
  local copies, waits for them, and re-layouts: 7.69 us -> 0 us
    pallas_call x0 -> x1, Pallas kernels: none -> 96.4 us  [body(): pl.pallas_call(store, out_shape=tuple((jax.ShapeDtypeStruct(r.shape, r.dt...]
    unnamed x12 -> x0, local copies, waits for them, and re-layouts: 7.69 us -> none
    pallas_call x1, Pallas kernels: 36.7 us -> 34.2 us  [body(): pl.pallas_call(functools.partial(kernel, nf, nphon), out_shape=(jax.Shape...]
where the time goes in v2:
time: 132 us
  Pallas kernels  131 us (99%)
    pallas_call x1, Pallas kernels, body(): pl.pallas_call(store, out_shape=tuple((jax.ShapeDtypeStruct(r.shape, r.dt...  96.4 us
    pallas_call x1, Pallas kernels, body(): pl.pallas_call(functools.partial(kernel, nf, nphon), out_shape=(jax.Shape...  34.2 us

profile of v2, /device:TPU:0, one launch (start us, length us, event | category | flops | bytes accessed | tf_op | source)
XLA Modules:
  0.0 131.9 jit_solution(15059357301227516123)
XLA Ops:
  1.3 34.2 %shard_map.84 = (bf16[512,512]{1,0:T(8,128)(2,1)}, bf16[512,512]{1,0:T(8,128)(2,1)}, f32[512,512]{1,0:T(8,128)}, f32[512,512]{1,0:T(8,128)}) custom-call(s32[1]{0:T(128)S(6)} %copy.9.band, bf16[512,512]{1,0:T(8,128)(2,1)} %q_hbm.1, bf16[512,512]{1,0:T(8,128)(2,1)} %k_hbm.1, bf16[512,512]{1,0:T(8,128)(2,1)} %v_hbm.1, bf16[512,512]{1,0:T(8,128)(2,1)} %g_hbm.1), custom_call_target="tpu_custom_call" | custom-call | tf_op jit(solution)/shard_map/pallas_call | solution.py:297
  35.5 96.4 %shard_map.85 = (bf16[512,512]{1,0:T(8,128)(2,1)}, bf16[512,512]{1,0:T(8,128)(2,1)}, f32[512,512]{1,0:T(8,128)}, f32[512,512]{1,0:T(8,128)}) custom-call(bf16[512,512]{1,0:T(8,128)(2,1)} %get-tuple-element.8.refs_0_, bf16[512,512]{1,0:T(8,128)(2,1)} %get-tuple-element.9.refs_1_, f32[512,512]{1,0:T(8,128)} %get-tuple-element.10.refs_2_, ...), custom_call_target="tpu_custom_call" | custom-call | tf_op jit(solution)/shard_map/pallas_call | solution.py:346

commit v3 on v2

--- a/solution.py
+++ b/solution.py
@@ -25,7 +25,7 @@
     band, q_hbm, k_hbm, v_hbm, g_hbm,
     al_hbm, gq_hbm, gk_hbm, gv_hbm,
     al_out, gq_out, gk_out, gv_out,
-    q, g, k, v, s, dp, prob, ds, o_part, gq_part, gk_part, gv_part,
+    q, g, k, v, o_raw, s, dp, prob, ds, o_part, gq_part, gk_part, gv_part,
     stat, stat_in, o_in1, o_sum, o_in2, q_in1, q_sum, q_in2, gk_in, gv_in,
     local_sem, store_sem, k_send, k_recv, v_send, v_recv, st_send, st_recv,
     o_send, o_recv, q_send, q_recv,
@@ -78,7 +78,6 @@
     first = jnp.zeros((1, nq), jnp.int32)
     for i in range(band.shape[0]):
         first = jnp.where(lane_tile == i, band[i], first)
-    ones = jnp.ones((8, width), BF16)
 
     def scores(t, top):
         r = pl.ds(pl.multiple_of(t * STEP, STEP), STEP)
@@ -109,6 +108,7 @@
         r = pl.ds(pl.multiple_of(t * STEP, STEP), STEP)
         e = jnp.exp(s[r, :] - top)
         s[r, :] = e
+        prob[r, :] = e.astype(BF16)
         tot = tot + jnp.sum(e.reshape(STEP // 8, 8, nq), axis=0)
         mix = mix + jnp.sum((e * dp[r, :]).reshape(STEP // 8, 8, nq), axis=0)
         return tot, mix
@@ -127,6 +127,7 @@
     ]
     for c in stats:
         c.start()
+    o_raw[...] = dot(prob[...], v[...], 0, 0)
     for c in stats:
         c.wait_recv()
     all_top = top
@@ -141,17 +142,8 @@
         delta = delta + stat_in[d - 1, 2:3, :] * w
     delta = delta / total
     mine = mine / total
-
-    def soften(t, carry):
-        r = pl.ds(pl.multiple_of(t * STEP, STEP), STEP)
-        pt = s[r, :] * mine
-        prob[r, :] = pt.astype(BF16)
-        d_s = pt * (dp[r, :] - delta)
-        dp[r, :] = d_s
-        ds[r, :] = d_s.astype(BF16)
-        return carry
-
-    lax.fori_loop(0, block // STEP, soften, 0)
+    column = jnp.swapaxes(jnp.broadcast_to(mine, (8, nq)), 0, 1)[:, 0:1]
+    o_part[...] = (o_raw[...] * column).astype(BF16)
 
     x, y = lax.rem(p, 2), p // 2
     xdev = {"phon": y * 2 + 1 - x}
@@ -217,11 +209,21 @@
         out[1].start()
         return out
 
-    o_part[...] = dot(prob[...], v[...], 0, 0).astype(BF16)
     o_1 = first_step(o_part, o_in1, o_send, o_recv)
+
+    def soften(t, carry):
+        r = pl.ds(pl.multiple_of(t * STEP, STEP), STEP)
+        pt = s[r, :] * mine
+        prob[r, :] = pt.astype(BF16)
+        d_s = pt * (dp[r, :] - delta)
+        dp[r, :] = d_s
+        ds[r, :] = d_s.astype(BF16)
+        return carry
+
+    lax.fori_loop(0, block // STEP, soften, 0)
+
     gq_part[...] = (dot(ds[...], k[...], 0, 0) * scale).astype(BF16)
     q_1 = first_step(gq_part, q_in1, q_send, q_recv)
-    o_2 = second_step(o_1, o_part, o_in1, o_sum, o_in2, o_send, o_recv)
 
     def key_grads(t, carry):
         t = lax.rem(t + near, block // STEP)
@@ -241,6 +243,7 @@
         back.append(remote(gv_part.at[slot], gv_in.at[d - 1], gv_send.at[d - 1], gv_recv.at[d - 1], fdev(-d)))
     for c in back:
         c.start()
+    o_2 = second_step(o_1, o_part, o_in1, o_sum, o_in2, o_send, o_recv)
     lax.fori_loop(far, block // STEP, key_grads, 0)
 
     q_2 = second_step(q_1, gq_part, q_in1, q_sum, q_in2, q_send, q_recv)
@@ -280,11 +283,16 @@
 
 
 def store(*refs):
-    n = len(refs) // 2
-    copies = [pltpu.make_async_copy(refs[i], refs[n + i], refs[-1].at[i]) for i in range(n)]
-    for c in copies:
-        c.start()
-    for c in copies:
+    n = (len(refs) - 2) // 3
+    srcs, dsts, bufs, (load_sem, store_sem) = refs[:n], refs[n:2 * n], refs[2 * n:3 * n], refs[3 * n:]
+    loads = [pltpu.make_async_copy(srcs[i], bufs[i], load_sem.at[i]) for i in range(n)]
+    stores = [pltpu.make_async_copy(bufs[i], dsts[i], store_sem.at[i]) for i in range(n)]
+    for c in loads:
+        c.start()
+    for c, d in zip(loads, stores):
+        c.wait()
+        d.start()
+    for c in stores:
         c.wait()
 
 
@@ -313,6 +321,7 @@
             pltpu.VMEM((nq, width), BF16),
             pltpu.VMEM((block, width), BF16),
             pltpu.VMEM((block, width), BF16),
+            pltpu.VMEM((nq, width), F32),
             pltpu.VMEM((block, nq), F32),
             pltpu.VMEM((block, nq), F32),
             pltpu.VMEM((block, nq), BF16),
@@ -348,7 +357,7 @@
         out_shape=tuple(jax.ShapeDtypeStruct(r.shape, r.dtype) for r in results),
         in_specs=[hbm] * 4,
         out_specs=(hbm,) * 4,
-        scratch_shapes=[dma((4,))],
+        scratch_shapes=[pltpu.VMEM(r.shape, r.dtype) for r in results] + [dma((4,))] * 2,
     )(*results)
 
 

time: 132 us -> 37.7 us (0.29)
  Pallas kernels: 131 us -> 36.2 us
    pallas_call x1, Pallas kernels: 96.4 us -> 2.93 us  [body(): pl.pallas_call(store, out_shape=tuple((jax.ShapeDtypeStruct(r.shape, r.dt...]
where the time goes in v3:
time: 37.7 us; the launch traced here: 37.5 us
  Pallas kernels  36.2 us (96%)
  between operations  1.29 us (3%)
    pallas_call x1, Pallas kernels, body(): pl.pallas_call(functools.partial(kernel, nf, nphon), out_shape=(jax.Shape...  33.3 us
    pallas_call x1, Pallas kernels, body(): pl.pallas_call(store, out_shape=tuple((jax.ShapeDtypeStruct(r.shape, r.dt...  2.93 us

profile of v3, /device:TPU:0, one launch (start us, length us, event | category | flops | bytes accessed | tf_op | source)
XLA Modules:
  0.0 37.5 jit_solution(14864060932187444756)
XLA Ops:
  1.3 33.3 %shard_map.84 = (bf16[512,512]{1,0:T(8,128)(2,1)}, bf16[512,512]{1,0:T(8,128)(2,1)}, f32[512,512]{1,0:T(8,128)}, f32[512,512]{1,0:T(8,128)}) custom-call(s32[1]{0:T(128)S(6)} %copy.9.band, bf16[512,512]{1,0:T(8,128)(2,1)} %q_hbm.1, bf16[512,512]{1,0:T(8,128)(2,1)} %k_hbm.1, bf16[512,512]{1,0:T(8,128)(2,1)} %v_hbm.1, bf16[512,512]{1,0:T(8,128)(2,1)} %g_hbm.1), custom_call_target="tpu_custom_call" | custom-call | tf_op jit(solution)/shard_map/pallas_call | solution.py:305
  34.6 2.9 %shard_map.85 = (bf16[512,512]{1,0:T(8,128)(2,1)}, bf16[512,512]{1,0:T(8,128)(2,1)}, f32[512,512]{1,0:T(8,128)}, f32[512,512]{1,0:T(8,128)}) custom-call(bf16[512,512]{1,0:T(8,128)(2,1)} %get-tuple-element.8.refs_0_, bf16[512,512]{1,0:T(8,128)(2,1)} %get-tuple-element.9.refs_1_, f32[512,512]{1,0:T(8,128)} %get-tuple-element.10.refs_2_, ...), custom_call_target="tpu_custom_call" | custom-call | tf_op jit(solution)/shard_map/pallas_call | solution.py:355
